TPU v7x, 32 devices: a whole 2x2x4 slice. The times are simulated.
32 devices in a mesh: row: 2 (over core), col: 4 (over z), rep: 4 (over y, x).
Axes of the slice: x: 2, y: 2, z: 4, core: 2. Of those that a mesh axis runs over, the one named last changes fastest.
Arguments:
- amplitudes: bfloat16 [1024, 4, 1792], P('row', 'rep', 'col'), may hold values from -6 to 6
- integrals: bfloat16 [4, 1792, 8, 512], P('rep', 'row', 'col'), may hold values from -0.0625 to 0.0625
- cycle_weight: bfloat16 [1792, 512], replicated, may hold values from -0.125 to 0.125
- amplitude_mask: int32 [8, 4, 14], replicated, may hold values 0 or 1
- integral_mask: int32 [4, 14, 8, 4], replicated, may hold values 0 or 1
- cycle_order: int32 [8], replicated, may hold values from 0 to 7, as said below
Outputs:
- ladder_residual: bfloat16 [1024, 8, 512], P(('row', 'rep'), 'col')
- cycle_residual: bfloat16 [1024, 4, 512], P(('row', 'col'), 'rep')
Inputs may be any that keep to these rules, and one draw needn't show every extreme that they name: cycle_order names every tile once; entries k * 4 to (k + 1) * 4 - 1 are a permutation of those same tile numbers.
All inputs are finite; a program needn't handle non-finite values.
Results may differ from a plain program's by a relative error of at most 0.0014.
Values may be sent and summed in bfloat16 or wider, within the bound.
A program may use at most 128 MiB of HBM per device.

v0:
```python
import jax
import jax.numpy as jnp
from jax import lax
from jax.sharding import PartitionSpec as P

TILE = 128


def contract_with(panel, piece):
    return jnp.einsum("pcn,cnaq->paq", panel, piece, preferred_element_type=jnp.float32)


def apply_cycle(cycle_weight, gathered):
    return jnp.einsum(
        "pcd,de->pce", gathered, cycle_weight, preferred_element_type=jnp.float32
    ).astype(jnp.bfloat16)


def body(amplitudes, integrals, cycle_weight, amplitude_mask, integral_mask, cycle_order):
    row_count = amplitudes.shape[0]
    d_local = amplitudes.shape[2]
    d_rows = integrals.shape[1]
    a_local = integrals.shape[2]
    row_index = lax.axis_index("row")
    col_index = lax.axis_index("col")
    rep_index = lax.axis_index("rep")
    amp_tiles = row_count // TILE
    zero_value = jnp.zeros((), jnp.bfloat16)
    mask_rows = lax.dynamic_slice(
        amplitude_mask,
        (row_index * amp_tiles, rep_index, 0),
        (amp_tiles, 1, amplitude_mask.shape[2]),
    )
    amp_expanded = jnp.repeat(jnp.repeat(mask_rows, TILE, axis=0), TILE, axis=2)
    amp_local_mask = lax.dynamic_slice_in_dim(amp_expanded, col_index * d_local, d_local, 2)
    local_amps = jnp.where(amp_local_mask > 0, amplitudes, zero_value)
    slab_tiles = lax.dynamic_slice(
        integral_mask,
        (rep_index, 0, col_index * a_local, 0),
        (1, integral_mask.shape[1], a_local, integral_mask.shape[3]),
    )
    slab_expanded = jnp.repeat(jnp.repeat(slab_tiles, TILE, axis=1), TILE, axis=3)
    slab_local_mask = lax.dynamic_slice_in_dim(slab_expanded, row_index * d_rows, d_rows, 1)
    local_ints = jnp.where(slab_local_mask > 0, integrals, zero_value)
    local_order = (
        lax.dynamic_slice_in_dim(cycle_order, row_index * amp_tiles, amp_tiles)
        - row_index * amp_tiles
    )
    spread = lax.all_to_all(local_amps, "rep", split_axis=0, concat_axis=1, tiled=True)
    panel = lax.all_gather(spread, "col", axis=2, tiled=True)
    all_slabs = lax.all_gather(local_ints, "rep", axis=0, tiled=True)
    totals = contract_with(panel, lax.all_gather(all_slabs, "row", axis=1, tiled=True))
    ladder = totals.astype(jnp.bfloat16)
    permuted = local_amps.reshape(amp_tiles, TILE, 1, d_local)[local_order].reshape(
        row_count, 1, d_local
    )
    cycle = apply_cycle(
        cycle_weight, lax.all_to_all(permuted, "col", split_axis=0, concat_axis=2, tiled=True)
    )
    return (ladder, cycle)


def solution(mesh):
    placed = (P("row", "rep", "col"), P("rep", "row", "col", None), P(), P(), P(), P())
    return jax.shard_map(
        body,
        mesh=mesh,
        in_specs=placed,
        out_specs=(P(("row", "rep"), "col", None), P(("row", "col"), "rep", None)),
        check_vma=False,
    )
```

profile of v0, /device:TPU:0, one launch (start us, length us, event | category | flops | bytes accessed | tf_op | source)
XLA Modules:
  0.0 208.3 jit_solution(9423440417677060962)
XLA Ops:
  7.2 0.8 dynamic-slice_bitcast_fusion
  8.3 5.8 %broadcast_in_dim.38 = s32[1792,2,4,128]{3,2,0,1:T(4,128)} broadcast(s32[1792,2,4]{2,0,1:T(8,128)S(1)} %bitcast.48), dimensions={0,1,2} | broadcast | bytes 7397376 | tf_op jit(solution)/shard_map/broadcast_in_dim | solution.py:42
  14.1 9.9 %broadcast_in_dim.39 = s32[1792,2,512]{2,0,1:T(8,128)} reshape(s32[1792,2,4,128]{3,2,0,1:T(4,128)} %broadcast_in_dim.38) | data formatting | bytes 14680064 | tf_op jit(solution)/shard_map/broadcast_in_dim | solution.py:42
  24.0 4.5 %fusion.1 = bf16[1,896,2,512]{3,1,0,2:T(8,128)(2,1)} fusion(s32[1792,2,512]{2,0,1:T(8,128)} %broadcast_in_dim.39, s32[]{:T(128)S(6)} %select_n.33, bf16[1,896,2,512]{3,2,1,0:T(2,128)(2,1)} %param.7), kind=kLoop, calls=%fused_computation.3 | loop fusion | flops 1835008 | bytes 7340036 | tf_op jit(solution)/shard_map/jit(_where)/select_n | solution.py:44
  28.6 0.7 constant_dynamic-slice_fusion
  29.5 0.5 broadcast_in_dim.33
  30.0 0.5 copy-done.1
  30.6 0.5 broadcast.28
  31.1 1.0 reduce
  32.1 0.2 copy.60
  32.3 0.6 reshape.58
  32.9 16.5 %all_to_all.33 = bf16[4,2,28672]{2,1,0:T(2,128)(2,1)} all-to-all(bf16[4,2,28672]{2,1,0:T(2,128)(2,1)S(1)} %reshape.58), channel_id=1, replica_groups=mesh['row'=2,'col'=4,'rep'=4] {'rep'}, dimensions={0} | all-to-all | bytes 917504 | tf_op jit(solution)/shard_map/all_to_all | solution.py:49
  49.4 2.4 %reshape.59 = bf16[512,1,448]{2,1,0:T(2,128)(2,1)S(1)} reshape(bf16[4,2,28672]{2,1,0:T(2,128)(2,1)} %all_to_all.33) | data formatting | bytes 917504
  51.8 0.9 copy.56
  52.7 2.0 copy.52
  54.8 57.6 %all-gather.5.cloned.1.call-done = bf16[4,896,2,512]{3,1,0,2:T(8,128)(2,1)} async-done(((bf16[1,896,2,512]{3,1,0,2:T(8,128)(2,1)}), bf16[4,896,2,512]{3,1,0,2:T(8,128)(2,1)}) %all-gather.5.cloned.1.call-update) | async-done | bytes 7340048 | tf_op jit(solution)/shard_map/all_gather | solution.py:51
  112.6 0.5 copy-done.2
  113.2 0.6 gather_fusion
  113.8 0.2 copy.53
  114.0 0.3 reshape.56
  114.4 4.0 %reduce.1 = bf16[512,448]{1,0:T(8,128)(2,1)S(1)} reduce(bf16[512,1,448]{2,1,0:T(2,128)(2,1)S(1)} %reshape.56, bf16[]{:T(256)} %broadcast.28), dimensions={1}, to_apply=%reshape.56.reduce_sub_computation | reduce | bytes 917506 | tf_op jit(solution)/shard_map/reshape | solution.py:54
  118.4 0.6 reshape.60
  119.0 29.7 %all_to_all.34 = bf16[4,2,28672]{2,1,0:T(2,128)(2,1)S(1)} all-to-all(bf16[4,2,28672]{2,1,0:T(2,128)(2,1)S(1)} %reshape.60), channel_id=1, replica_groups=mesh['row'=2,'col'=4,'rep'=4] {'col'}, dimensions={0} | all-to-all | bytes 917504 | tf_op jit(solution)/shard_map/all_to_all | solution.py:58
  148.7 0.7 reshape.61
  149.5 0.1 copy.57
  149.6 0.3 copy.54
  149.9 1.1 fusion.10
  151.0 14.2 %all-gather.9.cloned.1.call-done = bf16[128,4,1,1792]{0,1,2,3:T(4,128)(2,1)} async-done(((bf16[128,4,1,448]{0,1,2,3:T(4,128)(2,1)}), bf16[128,4,1,1792]{0,1,2,3:T(4,128)(2,1)}) %all-gather.9.cloned.1.call-update) | async-done | bytes 1835024 | tf_op jit(solution)/shard_map/all_gather | solution.py:50
  165.2 4.1 %copy.42 = bf16[128,4,1,1792]{3,0,1,2:T(8,128)(2,1)} copy(bf16[128,4,1,1792]{0,1,2,3:T(4,128)(2,1)} %all-gather.9.cloned.1.call-done) | data formatting | bytes 3670016 | tf_op jit(solution)/shard_map/all_gather | solution.py:50
  169.4 23.6 %all-gather.7.cloned.1.call-done = bf16[4,1792,2,512]{3,1,0,2:T(8,128)(2,1)} async-done(((bf16[4,896,2,512]{3,1,0,2:T(8,128)(2,1)}), bf16[4,1792,2,512]{3,1,0,2:T(8,128)(2,1)}) %all-gather.7.cloned.1.call-update) | async-done | bytes 14680080 | tf_op jit(solution)/shard_map/all_gather | solution.py:52
  193.0 7.8 %fusion.7 = bf16[128,2,512]{2,0,1:T(8,128)(2,1)S(1)} fusion(bf16[4,1792,2,512]{3,1,0,2:T(8,128)(2,1)} %all-gather.7.cloned.1.call-done, bf16[128,4,1,1792]{3,0,1,2:T(8,128)(2,1)} %copy.42), kind=kOutput, calls=%fused_computation.7 | convolution fusion | flops 1879179264 | bytes 16777216 | tf_op jit(solution)/shard_map/pcn,cnaq->paq/dot_general | solution.py:10
  200.8 1.0 copy.50
  (22 shorter events, 1.0 us)
Async XLA Ops:
  7.2 142.8 %copy-start = (bf16[1792,512]{1,0:T(8,128)(2,1)S(1)}, bf16[1792,512]{1,0:T(8,128)(2,1)}, u32[]{:S(2)}) copy-start(bf16[1792,512]{1,0:T(8,128)(2,1)} %param.8) | copy-start | bytes 5505028
  7.2 105.2 %all-gather.5.cloned.1.call-start = ((), (), s32[]{:S(2)}) async-start(), calls=%async_computation.2 | async-start | bytes 9175040 | tf_op jit(solution)/shard_map/all_gather | solution.py:51
  28.5 136.7 %all-gather.9.cloned.1.call-start = ((), (), s32[]{:S(2)}) async-start(), calls=%async_computation.4 | async-start | bytes 2293760 | tf_op jit(solution)/shard_map/all_gather | solution.py:50
  29.5 1.0 copy-start.1
  54.8 138.2 %all-gather.7.cloned.1.call-start = ((), (), s32[]{:S(2)}) async-start(), calls=%async_computation.3 | async-start | bytes 22020096 | tf_op jit(solution)/shard_map/all_gather | solution.py:52
  112.4 0.7 copy-start.2
Sparse Core Ops, SparseCore 0:
  28.6 83.7 all-gather.4
  114.0 51.2 all-gather.8
  166.8 26.1 all-gather.6
where the time goes:
time: 209 us; the launch traced here: 208 us
  waiting for transfers between devices  95.4 us (46%)
  blocking collectives  46.3 us (22%)
  local copies, waits for them, and re-layouts  34 us (16%)
  between operations  13.9 us (7%)
  other arithmetic  9.67 us (5%)
  matrix products  8.89 us (4%)
    all_gather x1, waiting for transfers between devices, body(): all_slabs = lax.all_gather(local_ints, 'rep', axis=0, tiled=True)  57.6 us
    all_to_all x1, blocking collectives, body(): lax.all_to_all(permuted, 'col', split_axis=0, concat_axis=2, tiled=True)  29.7 us
    all_gather x1, waiting for transfers between devices, body(): lax.all_gather(all_slabs, 'row', axis=1, tiled=True)  23.6 us
    all_to_all x1, blocking collectives, body(): lax.all_to_all(local_amps, 'rep', split_axis=0, concat_axis=1, tiled=True)  16.5 us
    broadcast_in_dim x2, local copies, waits for them, and re-layouts, body(): jnp.repeat(jnp.repeat(slab_tiles, TILE, axis=1), TILE, axis=3)  15.7 us
    all_gather x1, waiting for transfers between devices, body(): panel = lax.all_gather(spread, 'col', axis=2, tiled=True)  14.2 us
    dot_general x1, matrix products, contract_with(): jnp.einsum('pcn,cnaq->paq', panel, piece, preferred_element_type=jnp.floa...  7.79 us
    unnamed x17, local copies, waits for them, and re-layouts  7.63 us
  transfers between devices with their start and end apart: 3, of which 3 were waited for; matrix products, arithmetic and copies ran while one was open for 10% of the time, Pallas kernels for 0%

commit v1 on v0

--- a/solution.py
+++ b/solution.py
@@ -1,9 +1,16 @@
+import functools
+
 import jax
 import jax.numpy as jnp
 from jax import lax
+from jax.experimental import pallas as pl
+from jax.experimental.pallas import tpu as pltpu
 from jax.sharding import PartitionSpec as P
 
 TILE = 128
+HALF = TILE // 2
+MESH = pl.DeviceIdType.MESH
+VMEM_LIMIT = 40 * 2**20
 
 
 def contract_with(panel, piece):
@@ -60,12 +67,307 @@
     return (ladder, cycle)
 
 
+def fused_kernel(
+    cols,
+    amps_ref,
+    ints_ref,
+    weight_ref,
+    amp_mask,
+    int_mask,
+    order,
+    ladder_ref,
+    cycle_ref,
+    panel,
+    masked,
+    slab,
+    weight,
+    partial,
+    relayed,
+    incoming,
+    local_sem,
+    pair_sem,
+    send_sem,
+    recv_sem,
+    part_send,
+    part_recv,
+):
+    d_local = amps_ref.shape[0]
+    a_local, d_rows, width = ints_ref.shape
+    d_tiles = masked.shape[1] // TILE
+    b_tiles = width // TILE
+    tiles = masked.shape[0]
+    row, col, rep = (lax.axis_index(name) for name in ("row", "col", "rep"))
+    order_of = (3, 1, 2, 0)
+
+    barrier = pltpu.get_barrier_semaphore()
+    pl.semaphore_signal(barrier, inc=1, device_id={"row": 1 - row}, device_id_type=MESH)
+    for flip in order_of[:3]:
+        pl.semaphore_signal(barrier, inc=1, device_id={"rep": rep ^ flip}, device_id_type=MESH)
+
+    @pl.when(col > 0)
+    def _():
+        pl.semaphore_signal(barrier, inc=1, device_id={"col": col - 1}, device_id_type=MESH)
+
+    @pl.when(col < cols - 1)
+    def _():
+        pl.semaphore_signal(barrier, inc=1, device_id={"col": col + 1}, device_id_type=MESH)
+
+    def tile_of(k):
+        return rep ^ order_of[k]
+
+    def lanes(tile):
+        return pl.ds(pl.multiple_of(tile * TILE, TILE), TILE)
+
+    my_rows = pl.ds(pl.multiple_of(row * d_rows, TILE), d_rows)
+    copy_ints = pltpu.make_async_copy(ints_ref, slab.at[:, my_rows, :], local_sem.at[0])
+    copy_weight = pltpu.make_async_copy(weight_ref, weight, local_sem.at[1])
+    copy_amps = [
+        pltpu.make_async_copy(
+            amps_ref.at[:, lanes(tile_of(k))], panel.at[tile_of(k), col], local_sem.at[2 + k]
+        )
+        for k in range(tiles)
+    ]
+    for copy in [copy_amps[0], copy_ints] + copy_amps[1:] + [copy_weight]:
+        copy.start()
+
+    pl.semaphore_wait(barrier, 4 + (col > 0).astype(jnp.int32) + (col < cols - 1).astype(jnp.int32))
+
+    def hop(way, k, distance):
+        step = 1 if way == 0 else -1
+        source = col - step * distance
+        slot = panel.at[tile_of(k), source]
+        return pltpu.make_async_remote_copy(
+            src_ref=amps_ref.at[:, lanes(tile_of(k))] if distance == 0 else slot,
+            dst_ref=slot,
+            send_sem=send_sem.at[way, k, distance],
+            recv_sem=recv_sem.at[way, k, distance],
+            device_id={"col": col + step},
+            device_id_type=MESH,
+        )
+
+    def sends(way, distance):
+        if way == 0:
+            return (col >= distance) & (col < cols - 1)
+        return (col + distance < cols) & (col > 0)
+
+    def receives(way, distance):
+        return (col > distance) if way == 0 else (col + distance < cols - 1)
+
+    def start_hop(k, distance):
+        for way in range(2):
+            @pl.when(sends(way, distance))
+            def _():
+                hop(way, k, distance).start()
+
+    def start_own(k, busy):
+        for way in range(2):
+            forwards = col if way == 0 else cols - 1 - col
+
+            @pl.when(sends(way, 0) & ((forwards >= 2) if busy else (forwards < 2)))
+            def _():
+                hop(way, k, 0).start()
+
+    def await_hop(k, distance):
+        for way in range(2):
+            step = 1 if way == 0 else -1
+
+            @pl.when(receives(way, distance))
+            def _():
+                slot = panel.at[tile_of(k), col - step * (distance + 1)]
+                pltpu.make_async_remote_copy(
+                    src_ref=slot,
+                    dst_ref=slot,
+                    send_sem=send_sem.at[way, k, distance],
+                    recv_sem=recv_sem.at[way, k, distance],
+                    device_id={"col": col},
+                    device_id_type=MESH,
+                ).wait_recv()
+
+    start_hop(0, 0)
+    pair = pltpu.make_async_remote_copy(
+        src_ref=ints_ref,
+        dst_ref=slab.at[:, my_rows, :],
+        send_sem=pair_sem.at[0],
+        recv_sem=pair_sem.at[1],
+        device_id={"row": 1 - row},
+        device_id_type=MESH,
+    )
+    pair.start()
+
+    def part_copy(k, a):
+        if k == 0:
+            target, landing = rep ^ (1 + a), relayed.at[a]
+        else:
+            target, landing = rep ^ k, incoming.at[k - 1, a]
+        return pltpu.make_async_remote_copy(
+            src_ref=partial.at[k, a],
+            dst_ref=landing,
+            send_sem=part_send.at[k, a],
+            recv_sem=part_recv.at[k, a],
+            device_id={"rep": target},
+            device_id_type=MESH,
+        )
+
+    def pass_on(k, a):
+        part_copy(0, a).wait_recv()
+        partial[k, a] += relayed[a]
+        part_copy(k, a).start()
+
+    zero = jnp.zeros((TILE, TILE), jnp.bfloat16)
+
+    def mask_ints(tile, carry):
+        rows = pl.ds(pl.multiple_of(tile * TILE, TILE), TILE)
+        for a in range(a_local):
+            for b in range(b_tiles):
+                keep = int_mask[rep, col * a_local + a, b, tile] > 0
+                spot = pl.ds(b * TILE, TILE)
+                slab[a, rows, spot] = jnp.where(keep, slab[a, rows, spot], zero)
+        return carry
+
+    strip = jnp.zeros((HALF, TILE), jnp.bfloat16)
+
+    def block_product(k, source, first):
+        tile = tile_of(k)
+        for j in range(d_local // HALF):
+            keep = amp_mask[row * tiles + tile, rep, (source * d_local + j * HALF) // TILE] > 0
+            spot = pl.ds(pl.multiple_of(source * d_local + j * HALF, HALF), HALF)
+            masked[tile, spot, :] = jnp.where(
+                keep, panel[tile, source, pl.ds(j * HALF, HALF), :], strip
+            )
+        depth = pl.ds(pl.multiple_of(source * d_local, HALF), d_local)
+        for a in range(a_local):
+            product = lax.dot_general(
+                masked[tile, depth, :],
+                slab[a, depth, :],
+                (((0,), (0,)), ((), ())),
+                preferred_element_type=jnp.float32,
+            )
+            if first:
+                partial[k, a] = product
+            else:
+                partial[k, a] += product
+
+    for k in range(tiles):
+        if k + 1 < tiles:
+            start_own(k + 1, False)
+        copy_amps[k].wait()
+        if k > 0:
+            block_product(k, col, True)
+        for distance in range(cols - 1):
+            await_hop(k, distance)
+            if distance < cols - 2:
+                start_hop(k, distance + 1)
+            if distance == 0:
+                if k + 1 < tiles:
+                    start_own(k + 1, True)
+                if k == 0:
+                    copy_ints.wait()
+                    pair.wait()
+                    lax.fori_loop(0, d_tiles, mask_ints, 0)
+                    block_product(k, col, True)
+                if k == 2:
+                    pass_on(1, 1)
+            for way in range(2):
+                @pl.when(receives(way, distance))
+                def _():
+                    block_product(k, col - (1 if way == 0 else -1) * (distance + 1), False)
+        if k == 0:
+            part_copy(0, 0).start()
+            part_copy(0, 1).start()
+        elif k == 1:
+            part_copy(1, 0).start()
+        elif k == 2:
+            part_copy(2, 1).start()
+            pass_on(2, 0)
+
+    copy_weight.wait()
+    place = lax.rem(order[row * tiles + col], tiles)
+    cycle_ref[...] = lax.dot_general(
+        masked[place], weight[...], (((0,), (0,)), ((), ())), preferred_element_type=jnp.float32
+    ).astype(jnp.bfloat16)
+    for a in (0, 1):
+        part_copy(1, a).wait_recv()
+        partial[3, a] += incoming[0, a]
+    for a in (1, 0):
+        part_copy(2, a).wait_recv()
+        ladder_ref[a] = (partial[3, a] + incoming[1, a]).astype(jnp.bfloat16)
+    for k in range(tiles - 1):
+        for a in range(a_local):
+            part_copy(k, a).wait_send()
+    for k in range(tiles):
+        for distance in range(cols - 1):
+            for way in range(2):
+                @pl.when(sends(way, distance))
+                def _():
+                    hop(way, k, distance).wait_send()
+
+
+def fused_body(cols, amplitudes, integrals, cycle_weight, amplitude_mask, integral_mask, cycle_order):
+    rows, _, d_local = amplitudes.shape
+    _, d_rows, a_local, width = integrals.shape
+    depth = cols * d_local
+    tiles = rows // TILE
+    amps = jnp.transpose(amplitudes, (1, 2, 0)).reshape(d_local, rows)
+    ints = jnp.transpose(integrals, (0, 2, 1, 3)).reshape(a_local, d_rows, width)
+    anywhere = pl.BlockSpec(memory_space=pl.ANY)
+    scalars = pl.BlockSpec(memory_space=pltpu.SMEM)
+    in_vmem = pl.BlockSpec(memory_space=pltpu.VMEM)
+    ladder, cycle = pl.pallas_call(
+        functools.partial(fused_kernel, cols),
+        out_shape=(
+            jax.ShapeDtypeStruct((a_local, TILE, width), jnp.bfloat16),
+            jax.ShapeDtypeStruct((TILE, width), jnp.bfloat16),
+        ),
+        in_specs=[anywhere] * 3 + [scalars] * 3,
+        out_specs=(in_vmem, in_vmem),
+        scratch_shapes=[
+            pltpu.VMEM((tiles, cols, d_local, TILE), jnp.bfloat16),
+            pltpu.VMEM((tiles, depth, TILE), jnp.bfloat16),
+            pltpu.VMEM((a_local, depth, width), jnp.bfloat16),
+            pltpu.VMEM((depth, width), jnp.bfloat16),
+            pltpu.VMEM((tiles, a_local, TILE, width), jnp.float32),
+            pltpu.VMEM((a_local, TILE, width), jnp.float32),
+            pltpu.VMEM((2, a_local, TILE, width), jnp.float32),
+            pltpu.SemaphoreType.DMA((2 + tiles,)),
+            pltpu.SemaphoreType.DMA((2,)),
+            pltpu.SemaphoreType.DMA((2, tiles, cols - 1)),
+            pltpu.SemaphoreType.DMA((2, tiles, cols - 1)),
+            pltpu.SemaphoreType.DMA((tiles - 1, a_local)),
+            pltpu.SemaphoreType.DMA((tiles - 1, a_local)),
+        ],
+        compiler_params=pltpu.CompilerParams(
+            collective_id=0, has_side_effects=True, vmem_limit_bytes=VMEM_LIMIT
+        ),
+        name="ladder_and_cycle",
+    )(amps, ints, cycle_weight, amplitude_mask, jnp.transpose(integral_mask, (0, 2, 3, 1)), cycle_order)
+    return jnp.transpose(ladder, (1, 0, 2)), cycle[:, None, :]
+
+
+def fits_fused(mesh, amplitudes, integrals):
+    rows = amplitudes.shape[0] // mesh.shape["row"]
+    d_local = amplitudes.shape[2] // mesh.shape["col"]
+    return (
+        mesh.shape["row"] == 2
+        and mesh.shape["rep"] == 4
+        and rows == mesh.shape["rep"] * TILE
+        and rows == mesh.shape["col"] * TILE
+        and d_local % HALF == 0
+        and integrals.shape[2] == 2 * mesh.shape["col"]
+        and integrals.shape[1] // mesh.shape["row"] % TILE == 0
+    )
+
+
 def solution(mesh):
     placed = (P("row", "rep", "col"), P("rep", "row", "col", None), P(), P(), P(), P())
-    return jax.shard_map(
-        body,
-        mesh=mesh,
-        in_specs=placed,
-        out_specs=(P(("row", "rep"), "col", None), P(("row", "col"), "rep", None)),
-        check_vma=False,
-    )
+
+    def run(*arrays):
+        fused = fits_fused(mesh, *arrays[:2])
+        return jax.shard_map(
+            functools.partial(fused_body, mesh.shape["col"]) if fused else body,
+            mesh=mesh,
+            in_specs=placed,
+            out_specs=(P(("row", "rep"), "col", None), P(("row", "col"), "rep", None)),
+            check_vma=False,
+        )(*arrays)
+
+    return run

time: 209 us -> 50.8 us (0.24)
  waiting for transfers between devices: 95.4 us -> 0 us
  blocking collectives: 46.3 us -> 0 us
  Pallas kernels: 0 us -> 46.2 us
  local copies, waits for them, and re-layouts: 34 us -> 3.71 us
  between operations: 13.9 us -> 0.69 us
  other arithmetic: 9.67 us -> 0 us
  matrix products: 8.89 us -> 0 us
    all_gather x3 -> x0, waiting for transfers between devices: 95.4 us -> none  [the longest x1 57.6 us: body(): all_slabs = lax.all_gather(local_ints, 'rep', axis=0, tiled=True)]
    all_to_all x2 -> x0, blocking collectives: 46.3 us -> none  [the longest x1 29.7 us: body(): lax.all_to_all(permuted, 'col', split_axis=0, concat_axis=2, tiled=True)]
    pallas_call x0 -> x1, Pallas kernels: none -> 46.2 us  [fused_body(): pl.pallas_call(functools.partial(fused_kernel, cols), out_shape=(jax.Shap...]
    broadcast_in_dim x4 -> x0, local copies, waits for them, and re-layouts: 16.3 us -> none  [the longest x2 15.7 us: body(): jnp.repeat(jnp.repeat(slab_tiles, TILE, axis=1), TILE, axis=3)]
    dot_general x2 -> x0, matrix products: 8.89 us -> none  [the longest x1 7.79 us: contract_with(): jnp.einsum('pcn,cnaq->paq', panel, piece, preferred_element_type=jnp.floa...]
    select_n x4 -> x0, other arithmetic: 5.66 us -> none  [the longest x1 4.51 us: body(): local_ints = jnp.where(slab_local_mask > 0, integrals, zero_value)]
    all_gather x1 -> x0, local copies, waits for them, and re-layouts: 4.15 us -> none  [body(): panel = lax.all_gather(spread, 'col', axis=2, tiled=True)]
    reshape x1 -> x0, other arithmetic: 4 us -> none  [body(): local_amps.reshape(amp_tiles, TILE, 1, d_local)[local_order]]
  transfers between devices with their start and end apart: 3 -> 0, of which waited for: 3 -> 0; matrix products, arithmetic and copies ran while one was open for 10% -> 0% of each run, Pallas kernels for 0% -> 0%
where the time goes in v1:
time: 50.8 us; the launch traced here: 50.6 us
  Pallas kernels  46.2 us (91%)
  local copies, waits for them, and re-layouts  3.71 us (7%)
  between operations  0.69 us (1%)
    pallas_call x1, Pallas kernels, fused_body(): pl.pallas_call(functools.partial(fused_kernel, cols), out_shape=(jax.Shap...  46.2 us
    unnamed x13, local copies, waits for them, and re-layouts  3.71 us

profile of v1, /device:TPU:0, one launch (start us, length us, event | category | flops | bytes accessed | tf_op | source)
XLA Modules:
  0.0 50.6 jit_solution(424115164925131285)
XLA Ops:
  0.6 0.0 copy-start
  0.6 0.0 copy-start.1
  0.7 0.0 copy-start.2
  0.7 0.0 copy-start.3
  0.7 0.0 copy-start.4
  0.7 1.9 %copy.11 = bf16[1,896,2,512]{3,1,2,0:T(8,128)(2,1)S(1)} copy(bf16[1,896,2,512]{3,2,1,0:T(2,128)(2,1)} %param.7) | data formatting | bytes 3670016 | tf_op args[1]
  2.6 0.1 copy-done
  2.7 0.1 copy-done.1
  2.8 0.0 copy-done.2
  2.8 0.0 copy-done.3
  2.8 0.0 copy-done.4
  2.8 46.2 %ladder_and_cycle.1 = (bf16[2,128,512]{2,1,0:T(8,128)(2,1)S(1)}, bf16[128,512]{1,0:T(8,128)(2,1)S(1)}) custom-call(bf16[448,512]{1,0:T(8,128)(2,1)S(1)} %bitcast.12, bf16[2,896,512]{2,1,0:T(8,128)(2,1)S(1)} %bitcast.11, bf16[1792,512]{1,0:T(8,128)(2,1)S(1)} %copy-done, s32[8,4,14]{2,1,0:T(4,128)S(1)} %copy-done.3, s32[4,8,4,14]{3,2,1,0:T(4,128)S(1)} %bitcast.15, ...), custom_call_target="tpu_custom_call" | custom-call | tf_op jit(solution)/shard_map/ladder_and_cycle/pallas_call | solution.py:315
  49.0 1.0 %copy.9 = bf16[128,2,512]{2,1,0:T(2,128)(2,1)} copy(bf16[128,2,512]{2,0,1:T(8,128)(2,1)S(1)} %bitcast.13) | data formatting | bytes 524288
  50.0 0.7 %copy.13 = bf16[128,1,512]{2,0,1:T(8,128)(2,1)} copy(bf16[128,1,512]{2,0,1:T(8,128)(2,1)S(1)} %bitcast.14) | data formatting | bytes 262144
Async XLA Ops:
  0.6 2.1 %copy-start = (bf16[1792,512]{1,0:T(8,128)(2,1)S(1)}, bf16[1792,512]{1,0:T(8,128)(2,1)}, u32[]{:S(2)}) copy-start(bf16[1792,512]{1,0:T(8,128)(2,1)} %weight_ref.1) | copy-start | bytes 5505028
  0.6 2.1 %copy-start.1 = (bf16[512,1,448]{0,2,1:T(8,128)(2,1)S(1)}, bf16[512,1,448]{0,2,1:T(8,128)(2,1)}, u32[]{:S(2)}) copy-start(bf16[512,1,448]{0,2,1:T(8,128)(2,1)} %param.6) | copy-start | bytes 1376260
  0.7 2.1 %copy-start.2 = (s32[4,14,8,4]{1,3,2,0:T(4,128)S(1)}, s32[4,14,8,4]{1,3,2,0:T(4,128)}, u32[]{:S(2)}) copy-start(s32[4,14,8,4]{1,3,2,0:T(4,128)} %param.10) | copy-start | bytes 21508
  0.7 2.1 %copy-start.3 = (s32[8,4,14]{2,1,0:T(4,128)S(1)}, s32[8,4,14]{2,1,0:T(4,128)}, u32[]{:S(2)}) copy-start(s32[8,4,14]{2,1,0:T(4,128)} %amp_mask.1) | copy-start | bytes 5380
  0.7 2.1 %copy-start.4 = (s32[8]{0:T(128)S(1)}, s32[8]{0:T(128)}, u32[]{:S(2)}) copy-start(s32[8]{0:T(128)} %order.1) | copy-start | bytes 100

commit v2 on v1

--- a/solution.py
+++ b/solution.py
@@ -84,6 +84,8 @@
     partial,
     relayed,
     incoming,
+    chosen,
+    cycle_sum,
     local_sem,
     pair_sem,
     send_sem,
@@ -137,7 +139,7 @@
         source = col - step * distance
         slot = panel.at[tile_of(k), source]
         return pltpu.make_async_remote_copy(
-            src_ref=amps_ref.at[:, lanes(tile_of(k))] if distance == 0 else slot,
+            src_ref=slot,
             dst_ref=slot,
             send_sem=send_sem.at[way, k, distance],
             recv_sem=recv_sem.at[way, k, distance],
@@ -183,7 +185,10 @@
                     device_id_type=MESH,
                 ).wait_recv()
 
+    copy_amps[0].wait()
     start_hop(0, 0)
+    copy_amps[1].wait()
+    start_own(1, True)
     pair = pltpu.make_async_remote_copy(
         src_ref=ints_ref,
         dst_ref=slab.at[:, my_rows, :],
@@ -225,15 +230,17 @@
         return carry
 
     strip = jnp.zeros((HALF, TILE), jnp.bfloat16)
+    place = lax.rem(order[row * tiles + col], tiles)
+    copy_weight.wait()
 
     def block_product(k, source, first):
         tile = tile_of(k)
         for j in range(d_local // HALF):
             keep = amp_mask[row * tiles + tile, rep, (source * d_local + j * HALF) // TILE] > 0
             spot = pl.ds(pl.multiple_of(source * d_local + j * HALF, HALF), HALF)
-            masked[tile, spot, :] = jnp.where(
-                keep, panel[tile, source, pl.ds(j * HALF, HALF), :], strip
-            )
+            piece = jnp.where(keep, panel[tile, source, pl.ds(j * HALF, HALF), :], strip)
+            masked[tile, spot, :] = piece
+            chosen[spot, :] = jnp.where(place == tile, piece, strip if k == 0 else chosen[spot, :])
         depth = pl.ds(pl.multiple_of(source * d_local, HALF), d_local)
         for a in range(a_local):
             product = lax.dot_general(
@@ -246,19 +253,36 @@
                 partial[k, a] = product
             else:
                 partial[k, a] += product
+        if k == tiles - 1:
+            product = lax.dot_general(
+                chosen[depth, :],
+                weight[depth, :],
+                (((0,), (0,)), ((), ())),
+                preferred_element_type=jnp.float32,
+            )
+            if first:
+                cycle_sum[...] = product
+            else:
+                cycle_sum[...] += product
 
     for k in range(tiles):
         if k + 1 < tiles:
+            if k > 0:
+                copy_amps[k + 1].wait()
             start_own(k + 1, False)
-        copy_amps[k].wait()
         if k > 0:
             block_product(k, col, True)
         for distance in range(cols - 1):
+            if k == tiles - 1 and distance == cols - 2:
+                for sender in (1, 2):
+                    for a in range(a_local):
+                        part_copy(sender, a).wait_recv()
+                        partial[3, a] += incoming[sender - 1, a]
             await_hop(k, distance)
             if distance < cols - 2:
                 start_hop(k, distance + 1)
             if distance == 0:
-                if k + 1 < tiles:
+                if 0 < k < tiles - 1:
                     start_own(k + 1, True)
                 if k == 0:
                     copy_ints.wait()
@@ -280,17 +304,9 @@
             part_copy(2, 1).start()
             pass_on(2, 0)
 
-    copy_weight.wait()
-    place = lax.rem(order[row * tiles + col], tiles)
-    cycle_ref[...] = lax.dot_general(
-        masked[place], weight[...], (((0,), (0,)), ((), ())), preferred_element_type=jnp.float32
-    ).astype(jnp.bfloat16)
-    for a in (0, 1):
-        part_copy(1, a).wait_recv()
-        partial[3, a] += incoming[0, a]
-    for a in (1, 0):
-        part_copy(2, a).wait_recv()
-        ladder_ref[a] = (partial[3, a] + incoming[1, a]).astype(jnp.bfloat16)
+    cycle_ref[...] = cycle_sum[...].astype(jnp.bfloat16)
+    for a in range(a_local):
+        ladder_ref[a] = partial[3, a].astype(jnp.bfloat16)
     for k in range(tiles - 1):
         for a in range(a_local):
             part_copy(k, a).wait_send()
@@ -328,6 +344,8 @@
             pltpu.VMEM((tiles, a_local, TILE, width), jnp.float32),
             pltpu.VMEM((a_local, TILE, width), jnp.float32),
             pltpu.VMEM((2, a_local, TILE, width), jnp.float32),
+            pltpu.VMEM((depth, TILE), jnp.bfloat16),
+            pltpu.VMEM((TILE, width), jnp.float32),
             pltpu.SemaphoreType.DMA((2 + tiles,)),
             pltpu.SemaphoreType.DMA((2,)),
             pltpu.SemaphoreType.DMA((2, tiles, cols - 1)),

time: 50.8 us -> 50.2 us (0.988)
    pallas_call x1, Pallas kernels: 46.2 us -> 45.7 us  [fused_body(): pl.pallas_call(functools.partial(fused_kernel, cols), out_shape=(jax.Shap...]
where the time goes in v2:
time: 50.2 us; the launch traced here: 50.1 us
  Pallas kernels  45.7 us (91%)
  local copies, waits for them, and re-layouts  3.71 us (7%)
  between operations  0.69 us (1%)
    pallas_call x1, Pallas kernels, fused_body(): pl.pallas_call(functools.partial(fused_kernel, cols), out_shape=(jax.Shap...  45.7 us
    unnamed x13, local copies, waits for them, and re-layouts  3.71 us

profile of v2, /device:TPU:0, one launch (start us, length us, event | category | flops | bytes accessed | tf_op | source)
XLA Modules:
  0.0 50.1 jit_solution(14937855831990749572)
XLA Ops:
  0.6 0.0 copy-start
  0.6 0.0 copy-start.1
  0.7 0.0 copy-start.2
  0.7 0.0 copy-start.3
  0.7 0.0 copy-start.4
  0.7 1.9 %copy.11 = bf16[1,896,2,512]{3,1,2,0:T(8,128)(2,1)S(1)} copy(bf16[1,896,2,512]{3,2,1,0:T(2,128)(2,1)} %param.7) | data formatting | bytes 3670016 | tf_op args[1]
  2.6 0.1 copy-done
  2.7 0.1 copy-done.1
  2.8 0.0 copy-done.2
  2.8 0.0 copy-done.3
  2.8 0.0 copy-done.4
  2.8 45.7 %ladder_and_cycle.1 = (bf16[2,128,512]{2,1,0:T(8,128)(2,1)S(1)}, bf16[128,512]{1,0:T(8,128)(2,1)S(1)}) custom-call(bf16[448,512]{1,0:T(8,128)(2,1)S(1)} %bitcast.12, bf16[2,896,512]{2,1,0:T(8,128)(2,1)S(1)} %bitcast.11, bf16[1792,512]{1,0:T(8,128)(2,1)S(1)} %copy-done, s32[8,4,14]{2,1,0:T(4,128)S(1)} %copy-done.3, s32[4,8,4,14]{3,2,1,0:T(4,128)S(1)} %bitcast.15, ...), custom_call_target="tpu_custom_call" | custom-call | tf_op jit(solution)/shard_map/ladder_and_cycle/pallas_call | solution.py:331
  48.4 1.0 %copy.9 = bf16[128,2,512]{2,1,0:T(2,128)(2,1)} copy(bf16[128,2,512]{2,0,1:T(8,128)(2,1)S(1)} %bitcast.13) | data formatting | bytes 524288
  49.4 0.7 %copy.13 = bf16[128,1,512]{2,0,1:T(8,128)(2,1)} copy(bf16[128,1,512]{2,0,1:T(8,128)(2,1)S(1)} %bitcast.14) | data formatting | bytes 262144
Async XLA Ops:
  0.6 2.1 %copy-start = (bf16[1792,512]{1,0:T(8,128)(2,1)S(1)}, bf16[1792,512]{1,0:T(8,128)(2,1)}, u32[]{:S(2)}) copy-start(bf16[1792,512]{1,0:T(8,128)(2,1)} %weight_ref.1) | copy-start | bytes 5505028
  0.6 2.1 %copy-start.1 = (bf16[512,1,448]{0,2,1:T(8,128)(2,1)S(1)}, bf16[512,1,448]{0,2,1:T(8,128)(2,1)}, u32[]{:S(2)}) copy-start(bf16[512,1,448]{0,2,1:T(8,128)(2,1)} %param.6) | copy-start | bytes 1376260
  0.7 2.1 %copy-start.2 = (s32[4,14,8,4]{1,3,2,0:T(4,128)S(1)}, s32[4,14,8,4]{1,3,2,0:T(4,128)}, u32[]{:S(2)}) copy-start(s32[4,14,8,4]{1,3,2,0:T(4,128)} %param.10) | copy-start | bytes 21508
  0.7 2.1 %copy-start.3 = (s32[8,4,14]{2,1,0:T(4,128)S(1)}, s32[8,4,14]{2,1,0:T(4,128)}, u32[]{:S(2)}) copy-start(s32[8,4,14]{2,1,0:T(4,128)} %amp_mask.1) | copy-start | bytes 5380
  0.7 2.1 %copy-start.4 = (s32[8]{0:T(128)S(1)}, s32[8]{0:T(128)}, u32[]{:S(2)}) copy-start(s32[8]{0:T(128)} %order.1) | copy-start | bytes 100
